TPU v7x, 32 devices: a whole 2x2x4 slice. The times are simulated.
32 devices in a mesh: member: 4 (over z), lat: 4 (over y, core), lon: 2 (over x).
Axes of the slice: x: 2, y: 2, z: 4, core: 2. Of those that a mesh axis runs over, the one named last changes fastest.
Arguments:
- state: float32 [8, 5, 2, 128, 1024], P('member', None, None, 'lat', 'lon'), may hold values from -4 to 4
- kick: float32 [8, 5, 2, 128, 1024], P('member', None, None, 'lat', 'lon'), may hold values from -3 to 3
- forcing: float32 [5, 2, 128, 1024], P(None, None, 'lat', 'lon'), may hold values from -4 to 4
- coupling: float32 [2, 5, 5], replicated, may hold values from -3 to 3
- clone_src: int32 [8], replicated, may hold values from 0 to 7, as said below
Outputs:
- advanced: float32 [8, 5, 2, 128, 1024], P('member', None, None, 'lat', 'lon')
Inputs may be any that keep to these rules, and one draw needn't show every extreme that they name: `clone_src`: entry m equals m for a member that is kept; a replaced member names a member that is kept.
All inputs are finite; a program needn't handle non-finite values.
Results may differ from a plain program's by a relative error of at most 0.00012.
Values sent between devices are 32-bit elements; how exact they have to be, the bound alone decides.
No kernel may reach another device: no remote copies, remote signals or barrier semaphores. Data moves between devices by JAX's collectives and lax.ppermute only.
A program may use at most 128 MiB of HBM per device.

v0:
```python
import jax
import jax.numpy as jnp
from jax import lax
from jax.sharding import PartitionSpec as P

STEPS = 4


def with_halo(block, sides, width):
    for axis, dim in sides:
        count = lax.axis_size(axis)
        forward = [(i, i + 1) for i in range(count - 1)]
        forward.append((count - 1, 0))
        backward = [(target, source) for source, target in forward]
        low = lax.ppermute(
            lax.slice_in_dim(block, block.shape[dim] - width, None, axis=dim), axis, forward
        )
        high = lax.ppermute(lax.slice_in_dim(block, 0, width, axis=dim), axis, backward)
        block = jnp.concatenate([low, block, high], axis=dim)
    return block


def advance(padded, forcing_c, coupling):
    h = padded.shape[3] - 4
    w = padded.shape[4] - 4

    def part(di, dj):
        return padded[:, :, :, 2 + di : 2 + di + h, 2 + dj : 2 + dj + w]

    centre = part(0, 0)
    along_x = (8.0 * (part(0, 1) - part(0, -1)) - (part(0, 2) - part(0, -2))) / 12.0
    along_y = (8.0 * (part(1, 0) - part(-1, 0)) - (part(2, 0) - part(-2, 0))) / 12.0
    near = part(0, 1) + part(0, -1) + part(1, 0) + part(-1, 0)
    far_sum = part(0, 2) + part(0, -2) + part(2, 0) + part(-2, 0)
    laplace = (16.0 * near - far_sum - 60.0 * centre) / 12.0
    wind_u = centre[:, 0:1]
    wind_v = centre[:, 1:2]
    mixed = jnp.einsum("kvw,mwkij->mvkij", coupling, centre, precision=lax.Precision.HIGHEST)
    return centre + (
        -0.05 * (wind_u * along_x + wind_v * along_y)
        + 0.05 * laplace
        + 0.25 * mixed
        + 0.1 * forcing_c
    )


def shards(state, kick, forcing, coupling, clone_src):
    per_dev = state.shape[0]
    group = lax.axis_index("member")
    sources = lax.dynamic_slice_in_dim(clone_src, group * per_dev, per_dev)
    piece = lax.all_gather(state, "member", axis=0, tiled=True)
    count = piece.shape[0]
    inside = (sources >= 0) & (sources < count)
    rows = jnp.take(piece, jnp.clip(sources, 0, count - 1), axis=0)
    field = jnp.where(inside[:, None, None, None, None], rows, jnp.zeros_like(state))
    field = field + kick
    lat_dev = state.shape[3]
    lat_total = lat_dev * lax.axis_size("lat")
    base = lax.axis_index("lat") * lat_dev

    def zero_rows(values, first_row):
        rows = first_row + jnp.arange(values.shape[3], dtype=jnp.int32)
        keep = (rows >= 0) & (rows < lat_total)
        return jnp.where(keep[:, None], values, 0.0)

    for step in range(STEPS):
        padded = with_halo(field, (("lat", 3), ("lon", 4)), 2)
        padded = zero_rows(padded, base - 2)
        field = advance(padded, forcing, coupling)
    return field


def solution(mesh):
    in_specs = (
        P("member", None, None, "lat", "lon"),
        P("member", None, None, "lat", "lon"),
        P(None, None, "lat", "lon"),
        P(),
        P(),
    )
    out_specs = P("member", None, None, "lat", "lon")
    return jax.shard_map(shards, mesh=mesh, in_specs=in_specs, out_specs=out_specs, check_vma=False)
```

profile of v0, /device:TPU:17, one launch (start us, length us, event | category | flops | bytes accessed | tf_op | source)
XLA Modules:
  0.0 208.6 jit_solution(15952054877368690892)
XLA Ops:
  6.5 0.7 all-gather.2.cloned.1.call-update
  7.3 0.7 compare_and_fusion
  8.0 98.5 %all-gather.2.cloned.1.call-done = f32[8,5,2,32,512]{4,3,2,1,0:T(8,128)} async-done(((f32[2,5,2,32,512]{4,3,2,1,0:T(8,128)}), f32[8,5,2,32,512]{4,3,2,1,0:T(8,128)}) %all-gather.2.cloned.1.call-update) | async-done | bytes 5242896 | tf_op jit(solution)/shard_map/all_gather | solution.py:51
  106.5 3.1 %gather_fusion = f32[2,5,2,32,512]{4,3,2,1,0:T(8,128)S(1)} fusion(f32[8,5,2,32,512]{4,3,2,1,0:T(8,128)} %all-gather.2.cloned.1.call-done, s32[1024]{0:T(1024)S(1)} %pad_clamp_fusion), kind=kCustom, calls=%fused_computation | custom fusion | bytes 2621448 | tf_op jit(solution)/shard_map/jit(_take)/gather | solution.py:54
  109.6 3.9 %copy_add_fusion = f32[2,5,2,32,512]{4,1,3,0,2:T(8,128)S(1)} fusion(f32[2,5,2,32,512]{4,3,2,1,0:T(8,128)} %param.6, f32[2,5,2,32,512]{4,3,2,1,0:T(8,128)S(1)} %gather_fusion, pred[2]{0:T(512)(128)(4,1)S(1)} %get-tuple-element.5, pred[2]{0:T(512)(128)(4,1)S(1)} %get-tuple-element.31), kind=kLoop, calls=%fused_computation.17 | loop fusion | flops 983040 | bytes 3932164 | tf_op jit(solution)/shard_map/add | solution.py:56
  113.5 1.8 collective-permute-start
  115.4 2.4 %collective-permute-done = f32[2,5,2,2,512]{4,1,3,0,2:T(8,128)S(1)} collective-permute-done((f32[2,5,2,2,512]{4,1,3,0,2:T(8,128)S(1)}, f32[2,5,2,2,512]{4,1,3,0,2:T(8,128)S(1)}, u32[]{:S(2)}, u32[]{:S(2)}) %collective-permute-start) | collective-permute-done | bytes 81952 | tf_op jit(solution)/shard_map/ppermute | solution.py:15
  117.8 2.0 collective-permute-done.1
  119.8 1.8 pad_maximum_fusion.11
  121.6 1.3 copy.23
  122.9 0.3 copy.24
  123.2 1.2 collective-permute-start.3
  124.4 0.3 collective-permute-start.2
  124.7 1.4 copy.28
  126.1 1.4 collective-permute-done.2
  127.5 0.4 copy.25
  127.8 0.4 copy.26
  128.2 1.9 maximum_select_fusion
  130.2 1.1 slice_multiply_fusion.7
  131.4 6.2 %fusion.7 = f32[2,5,2,32,512]{4,1,3,0,2:T(8,128)S(1)} fusion(f32[2,5,2,36,516]{4,1,3,0,2:T(8,128)S(1)} %maximum_select_fusion, f32[5,2,32,512]{3,0,2,1:T(8,128)S(1)} %copy-done.1, f32[2,2,32,512]{3,2,0,1:T(8,128)S(1)} %get-tuple-element.32, f32[2,2,32,512]{3,2,0,1:T(8,128)S(1)} %get-tuple-element.33, f32[2,5,5,1,1]{2,0,1,4,3:T(2,128)S(1)} %bitcast.50), kind=kOutput, calls=%fused_computation.16 | convolution fusion | flops 28835840 | bytes 23860224 | tf_op jit(solution)/shard_map/kvw,mwkij->mvkij/dot_general | solution.py:38
  137.6 1.5 collective-permute-start.4
  139.2 2.5 %collective-permute-done.4 = f32[2,5,2,2,512]{4,1,3,0,2:T(8,128)S(1)} collective-permute-done((f32[2,5,2,2,512]{4,1,3,0,2:T(8,128)S(1)}, f32[2,5,2,2,512]{4,1,3,0,2:T(8,128)S(1)}, u32[]{:S(2)}, u32[]{:S(2)}) %collective-permute-start.4) | collective-permute-done | bytes 81952 | tf_op jit(solution)/shard_map/ppermute | solution.py:15
  141.7 1.9 collective-permute-done.5
  143.6 0.2 pad_maximum_fusion.8
  143.8 0.8 copy.29
  144.7 0.3 collective-permute-start.6
  144.9 0.3 copy.30
  145.2 1.2 collective-permute-start.7
  146.4 1.1 collective-permute-done.6
  147.6 0.4 copy.31
  147.9 0.5 collective-permute-done.7
  148.4 1.1 copy.32
  149.5 1.1 maximum_select_fusion.1
  150.6 1.1 slice_multiply_fusion.5
  151.8 6.2 %fusion.5 = f32[2,5,2,32,512]{4,1,3,0,2:T(8,128)S(1)} fusion(f32[2,5,2,36,516]{4,1,3,0,2:T(8,128)S(1)} %maximum_select_fusion.1, f32[2,2,32,512]{3,2,0,1:T(8,128)S(1)} %bitcast.58, f32[2,2,32,512]{3,2,0,1:T(8,128)S(1)} %bitcast.55, f32[5,2,32,512]{3,0,2,1:T(8,128)S(1)} %copy-done.2, f32[2,5,5,1,1]{2,0,1,4,3:T(2,128)S(1)} %bitcast.53), kind=kOutput, calls=%fused_computation.13 | convolution fusion | flops 28835840 | bytes 23860224 | tf_op jit(solution)/shard_map/kvw,mwkij->mvkij/dot_general | solution.py:38
  158.1 1.6 collective-permute-start.8
  159.7 2.5 %collective-permute-done.8 = f32[2,5,2,2,512]{4,1,3,0,2:T(8,128)S(1)} collective-permute-done((f32[2,5,2,2,512]{4,1,3,0,2:T(8,128)S(1)}, f32[2,5,2,2,512]{4,1,3,0,2:T(8,128)S(1)}, u32[]{:S(2)}, u32[]{:S(2)}) %collective-permute-start.8) | collective-permute-done | bytes 81952 | tf_op jit(solution)/shard_map/ppermute | solution.py:15
  162.2 1.9 collective-permute-done.9
  164.3 0.8 copy.34
  165.2 1.2 collective-permute-start.10
  166.4 0.3 copy.35
  166.6 0.3 collective-permute-start.11
  166.9 1.1 collective-permute-done.10
  168.1 0.4 copy.36
  168.4 1.4 collective-permute-done.11
  169.9 1.1 copy.37
  170.9 1.1 maximum_select_fusion.2
  172.0 1.1 slice_multiply_fusion.3
  173.2 6.2 %fusion.3 = f32[2,5,2,32,512]{4,1,3,0,2:T(8,128)S(1)} fusion(f32[2,5,2,36,516]{4,1,3,0,2:T(8,128)S(1)} %maximum_select_fusion.2, f32[2,2,32,512]{3,2,0,1:T(8,128)S(1)} %bitcast.59, f32[2,2,32,512]{3,2,0,1:T(8,128)S(1)} %bitcast.56, f32[5,2,32,512]{3,0,2,1:T(8,128)S(1)} %copy-done.3, f32[2,5,5,1,1]{2,0,1,4,3:T(2,128)S(1)} %bitcast.52), kind=kOutput, calls=%fused_computation.10 | convolution fusion | flops 28835840 | bytes 23860224 | tf_op jit(solution)/shard_map/kvw,mwkij->mvkij/dot_general | solution.py:38
  179.5 1.7 collective-permute-start.12
  181.2 2.6 %collective-permute-done.12 = f32[2,5,2,2,512]{4,1,3,0,2:T(8,128)S(1)} collective-permute-done((f32[2,5,2,2,512]{4,1,3,0,2:T(8,128)S(1)}, f32[2,5,2,2,512]{4,1,3,0,2:T(8,128)S(1)}, u32[]{:S(2)}, u32[]{:S(2)}) %collective-permute-start.12) | collective-permute-done | bytes 81952 | tf_op jit(solution)/shard_map/ppermute | solution.py:15
  183.7 1.8 collective-permute-done.13
  185.8 0.8 copy.39
  186.6 0.3 collective-permute-start.14
  186.9 0.3 copy.40
  187.1 1.2 collective-permute-start.15
  188.4 1.1 collective-permute-done.14
  189.5 0.4 copy.41
  189.9 0.5 collective-permute-done.15
  190.4 1.1 copy.42
  191.5 1.1 maximum_select_fusion.3
  192.5 1.1 slice_multiply_fusion.1
  193.8 6.2 %fusion.1 = f32[2,5,2,32,512]{4,1,3,0,2:T(8,128)S(1)} fusion(f32[2,5,2,36,516]{4,1,3,0,2:T(8,128)S(1)} %maximum_select_fusion.3, f32[2,2,32,512]{3,2,0,1:T(8,128)S(1)} %bitcast.57, f32[2,2,32,512]{3,2,0,1:T(8,128)S(1)} %bitcast.54, f32[5,2,32,512]{3,0,2,1:T(8,128)S(1)} %copy-done.4, f32[2,5,5,1,1]{2,0,1,4,3:T(2,128)S(1)} %bitcast.51), kind=kOutput, calls=%fused_computation.7 | convolution fusion | flops 28835840 | bytes 23860224 | tf_op jit(solution)/shard_map/kvw,mwkij->mvkij/dot_general | solution.py:38
  200.0 1.8 copy.44
  (34 shorter events, 0.8 us)
Async XLA Ops:
  6.5 124.8 %copy-start = (f32[2,5,5]{2,0,1:T(2,128)S(1)}, f32[2,5,5]{2,0,1:T(2,128)}, u32[]{:S(2)}) copy-start(f32[2,5,5]{2,0,1:T(2,128)} %param.8) | copy-start | bytes 604
  6.5 99.9 %all-gather.2.cloned.1.call-start = ((), (), s32[]{:S(2)}) async-start(), calls=%async_computation | async-start | bytes 6553600 | tf_op jit(solution)/shard_map/all_gather | solution.py:51
  109.6 5.7 %copy-start.5 = (f32[5,2,32,512]{3,2,1,0:T(8,128)S(1)}, f32[5,2,32,512]{3,2,1,0:T(8,128)}, u32[]{:S(2)}) copy-start(f32[5,2,32,512]{3,2,1,0:T(8,128)} %param.7) | copy-start | bytes 1966084
  113.5 4.3 %collective-permute-start = (f32[2,5,2,2,512]{4,1,3,0,2:T(8,128)S(1)}, f32[2,5,2,2,512]{4,1,3,0,2:T(8,128)S(1)}, u32[]{:S(2)}, u32[]{:S(2)}) collective-permute-start(f32[2,5,2,2,512]{4,1,3,0,2:T(8,128)S(1)} %get-tuple-element.29), channel_id=1, source_target_pairs={{0,2},{2,4},{4,6},{6,0},{1,3},{3,5},{5,7},{7,1},{8,10},{10,12},{12... | collective-permute-start | bytes 245768 | tf_op jit(solution)/shard_map/ppermute | solution.py:15
  115.3 4.5 %collective-permute-start.1 = (f32[2,5,2,2,512]{4,1,3,0,2:T(8,128)S(1)}, f32[2,5,2,2,512]{4,1,3,0,2:T(8,128)}, u32[]{:S(2)}, u32[]{:S(2)}) collective-permute-start(f32[2,5,2,2,512]{4,1,3,0,2:T(8,128)S(1)} %get-tuple-element.30), channel_id=1, source_target_pairs={{2,0},{4,2},{6,4},{0,6},{3,1},{5,3},{7,5},{1,7},{10,8},{12,10},{14... | collective-permute-start | bytes 245768 | tf_op jit(solution)/shard_map/ppermute | solution.py:18
  123.2 4.7 %collective-permute-start.3 = (f32[2,5,2,36,2]{3,4,2,1,0:T(2,128)S(1)}, f32[2,5,2,36,2]{3,4,2,1,0:T(2,128)S(1)}, u32[]{:S(2)}, u32[]{:S(2)}) collective-permute-start(f32[2,5,2,36,2]{3,4,2,1,0:T(2,128)S(1)} %copy.24), channel_id=1, source_target_pairs={{1,0},{0,1},{3,2},{2,3},{5,4},{4,5},{7,6},{6,7},{9,8},{8,9},{11,10... | collective-permute-start | bytes 17288 | tf_op jit(solution)/shard_map/ppermute | solution.py:18
  124.4 3.0 %collective-permute-start.2 = (f32[2,5,2,36,2]{3,4,2,1,0:T(2,128)S(1)}, f32[2,5,2,36,2]{3,4,2,1,0:T(2,128)S(1)}, u32[]{:S(2)}, u32[]{:S(2)}) collective-permute-start(f32[2,5,2,36,2]{3,4,2,1,0:T(2,128)S(1)} %copy.23), channel_id=1, source_target_pairs={{0,1},{1,0},{2,3},{3,2},{4,5},{5,4},{6,7},{7,6},{8,9},{9,8},{10,11... | collective-permute-start | bytes 17288 | tf_op jit(solution)/shard_map/ppermute | solution.py:15
  130.1 1.2 copy-start.1
  137.6 4.0 %collective-permute-start.4 = (f32[2,5,2,2,512]{4,1,3,0,2:T(8,128)S(1)}, f32[2,5,2,2,512]{4,1,3,0,2:T(8,128)S(1)}, u32[]{:S(2)}, u32[]{:S(2)}) collective-permute-start(f32[2,5,2,2,512]{4,1,3,0,2:T(8,128)S(1)} %get-tuple-element.27), channel_id=1, source_target_pairs={{0,2},{2,4},{4,6},{6,0},{1,3},{3,5},{5,7},{7,1},{8,10},{10,12},{12... | collective-permute-start | bytes 245768 | tf_op jit(solution)/shard_map/ppermute | solution.py:15
  139.2 4.4 %collective-permute-start.5 = (f32[2,5,2,2,512]{4,1,3,0,2:T(8,128)S(1)}, f32[2,5,2,2,512]{4,1,3,0,2:T(8,128)S(1)}, u32[]{:S(2)}, u32[]{:S(2)}) collective-permute-start(f32[2,5,2,2,512]{4,1,3,0,2:T(8,128)S(1)} %get-tuple-element.28), channel_id=1, source_target_pairs={{2,0},{4,2},{6,4},{0,6},{3,1},{5,3},{7,5},{1,7},{10,8},{12,10},{14... | collective-permute-start | bytes 245768 | tf_op jit(solution)/shard_map/ppermute | solution.py:18
  144.7 2.9 %collective-permute-start.6 = (f32[2,5,2,36,2]{3,4,2,1,0:T(2,128)}, f32[2,5,2,36,2]{3,4,2,1,0:T(2,128)S(1)}, u32[]{:S(2)}, u32[]{:S(2)}) collective-permute-start(f32[2,5,2,36,2]{3,4,2,1,0:T(2,128)} %copy.29), channel_id=1, source_target_pairs={{0,1},{1,0},{2,3},{3,2},{4,5},{5,4},{6,7},{7,6},{8,9},{9,8},{10,11... | collective-permute-start | bytes 17288 | tf_op jit(solution)/shard_map/ppermute | solution.py:15
  145.2 3.3 %collective-permute-start.7 = (f32[2,5,2,36,2]{3,4,2,1,0:T(2,128)S(1)}, f32[2,5,2,36,2]{3,4,2,1,0:T(2,128)}, u32[]{:S(2)}, u32[]{:S(2)}) collective-permute-start(f32[2,5,2,36,2]{3,4,2,1,0:T(2,128)S(1)} %copy.30), channel_id=1, source_target_pairs={{1,0},{0,1},{3,2},{2,3},{5,4},{4,5},{7,6},{6,7},{9,8},{8,9},{11,10... | collective-permute-start | bytes 17288 | tf_op jit(solution)/shard_map/ppermute | solution.py:18
  150.6 1.2 copy-start.2
  158.1 4.2 %collective-permute-start.8 = (f32[2,5,2,2,512]{4,1,3,0,2:T(8,128)S(1)}, f32[2,5,2,2,512]{4,1,3,0,2:T(8,128)S(1)}, u32[]{:S(2)}, u32[]{:S(2)}) collective-permute-start(f32[2,5,2,2,512]{4,1,3,0,2:T(8,128)S(1)} %get-tuple-element.25), channel_id=1, source_target_pairs={{0,2},{2,4},{4,6},{6,0},{1,3},{3,5},{5,7},{7,1},{8,10},{10,12},{12... | collective-permute-start | bytes 245768 | tf_op jit(solution)/shard_map/ppermute | solution.py:15
  159.7 4.4 %collective-permute-start.9 = (f32[2,5,2,2,512]{4,1,3,0,2:T(8,128)S(1)}, f32[2,5,2,2,512]{4,1,3,0,2:T(8,128)S(1)}, u32[]{:S(2)}, u32[]{:S(2)}) collective-permute-start(f32[2,5,2,2,512]{4,1,3,0,2:T(8,128)S(1)} %get-tuple-element.26), channel_id=1, source_target_pairs={{2,0},{4,2},{6,4},{0,6},{3,1},{5,3},{7,5},{1,7},{10,8},{12,10},{14... | collective-permute-start | bytes 245768 | tf_op jit(solution)/shard_map/ppermute | solution.py:18
  165.2 2.9 %collective-permute-start.10 = (f32[2,5,2,36,2]{3,4,2,1,0:T(2,128)}, f32[2,5,2,36,2]{3,4,2,1,0:T(2,128)S(1)}, u32[]{:S(2)}, u32[]{:S(2)}) collective-permute-start(f32[2,5,2,36,2]{3,4,2,1,0:T(2,128)} %copy.34), channel_id=1, source_target_pairs={{0,1},{1,0},{2,3},{3,2},{4,5},{5,4},{6,7},{7,6},{8,9},{9,8},{10,11... | collective-permute-start | bytes 17288 | tf_op jit(solution)/shard_map/ppermute | solution.py:15
  166.6 3.3 %collective-permute-start.11 = (f32[2,5,2,36,2]{3,4,2,1,0:T(2,128)S(1)}, f32[2,5,2,36,2]{3,4,2,1,0:T(2,128)}, u32[]{:S(2)}, u32[]{:S(2)}) collective-permute-start(f32[2,5,2,36,2]{3,4,2,1,0:T(2,128)S(1)} %copy.35), channel_id=1, source_target_pairs={{1,0},{0,1},{3,2},{2,3},{5,4},{4,5},{7,6},{6,7},{9,8},{8,9},{11,10... | collective-permute-start | bytes 17288 | tf_op jit(solution)/shard_map/ppermute | solution.py:18
  172.0 1.2 copy-start.3
  179.5 4.2 %collective-permute-start.12 = (f32[2,5,2,2,512]{4,1,3,0,2:T(8,128)S(1)}, f32[2,5,2,2,512]{4,1,3,0,2:T(8,128)S(1)}, u32[]{:S(2)}, u32[]{:S(2)}) collective-permute-start(f32[2,5,2,2,512]{4,1,3,0,2:T(8,128)S(1)} %get-tuple-element.23), channel_id=1, source_target_pairs={{0,2},{2,4},{4,6},{6,0},{1,3},{3,5},{5,7},{7,1},{8,10},{10,12},{12... | collective-permute-start | bytes 245768 | tf_op jit(solution)/shard_map/ppermute | solution.py:15
  181.2 4.4 %collective-permute-start.13 = (f32[2,5,2,2,512]{4,1,3,0,2:T(8,128)S(1)}, f32[2,5,2,2,512]{4,1,3,0,2:T(8,128)S(1)}, u32[]{:S(2)}, u32[]{:S(2)}) collective-permute-start(f32[2,5,2,2,512]{4,1,3,0,2:T(8,128)S(1)} %get-tuple-element.24), channel_id=1, source_target_pairs={{2,0},{4,2},{6,4},{0,6},{3,1},{5,3},{7,5},{1,7},{10,8},{12,10},{14... | collective-permute-start | bytes 245768 | tf_op jit(solution)/shard_map/ppermute | solution.py:18
  186.6 2.9 %collective-permute-start.14 = (f32[2,5,2,36,2]{3,4,2,1,0:T(2,128)}, f32[2,5,2,36,2]{3,4,2,1,0:T(2,128)S(1)}, u32[]{:S(2)}, u32[]{:S(2)}) collective-permute-start(f32[2,5,2,36,2]{3,4,2,1,0:T(2,128)} %copy.39), channel_id=1, source_target_pairs={{0,1},{1,0},{2,3},{3,2},{4,5},{5,4},{6,7},{7,6},{8,9},{9,8},{10,11... | collective-permute-start | bytes 17288 | tf_op jit(solution)/shard_map/ppermute | solution.py:15
  187.1 3.3 %collective-permute-start.15 = (f32[2,5,2,36,2]{3,4,2,1,0:T(2,128)S(1)}, f32[2,5,2,36,2]{3,4,2,1,0:T(2,128)}, u32[]{:S(2)}, u32[]{:S(2)}) collective-permute-start(f32[2,5,2,36,2]{3,4,2,1,0:T(2,128)S(1)} %copy.40), channel_id=1, source_target_pairs={{1,0},{0,1},{3,2},{2,3},{5,4},{4,5},{7,6},{6,7},{9,8},{8,9},{11,10... | collective-permute-start | bytes 17288 | tf_op jit(solution)/shard_map/ppermute | solution.py:18
  192.5 1.2 copy-start.4
Sparse Core Ops, SparseCore 0:
  8.9 97.5 all-gather.1
where the time goes:
time: 212 us; the launch traced here: 209 us
  waiting for transfers between devices  124 us (58%)
  matrix products  24.9 us (12%)
  other arithmetic  16.9 us (8%)
  local copies, waits for them, and re-layouts  16.4 us (8%)
  between operations  13.7 us (6%)
  starting transfers between devices  12.7 us (6%)
    all_gather x1, waiting for transfers between devices, shards(): piece = lax.all_gather(state, 'member', axis=0, tiled=True)  98.5 us
    dot_general x4, matrix products, advance(): jnp.einsum('kvw,mwkij->mvkij', coupling, centre, precision=lax.Precision....  24.9 us
    ppermute x8, waiting for transfers between devices, with_halo(): lax.ppermute(lax.slice_in_dim(block, block.shape[dim] - width, None, axis...  14.8 us
    ppermute x8, waiting for transfers between devices, with_halo(): lax.ppermute(lax.slice_in_dim(block, 0, width, axis=dim), axis, backward)  10 us
    ppermute x8, starting transfers between devices, with_halo(): lax.ppermute(lax.slice_in_dim(block, block.shape[dim] - width, None, axis...  8.64 us
    select_n x4, other arithmetic, zero_rows(): return jnp.where(keep[:, None], values, 0.0)  5.13 us
    mul x4, other arithmetic, advance(): wind_u * along_x + wind_v * along_y  4.59 us
  transfers between devices with their start and end apart: 17, of which 16 were waited for; matrix products, arithmetic and copies ran while one was open for 2% of the time, Pallas kernels for 0%

commit v1 on v0

v1 whole, which is shorter than its diff:
```python
import functools

import jax
import jax.numpy as jnp
from jax import lax
from jax.experimental import pallas as pl
from jax.experimental.pallas import tpu as pltpu
from jax.sharding import PartitionSpec as P

STEPS = 4
REACH = 2
HALO = STEPS * REACH
LANES = 128
ROWS = 8
SPAN = LANES - 2 * HALO
K = 0.05 / 12.0
VMEM = 48 * 1024 * 1024


def lane_index(shape):
    return lax.broadcasted_iota(jnp.int32, shape, len(shape) - 1)


def turn(x, shift):
    shift = shift % LANES
    return x if shift == 0 else pltpu.roll(x, shift, x.ndim - 1)


def edge_kernel(field_ref, kick_ref, forcing_ref, start_ref, top_ref, bottom_ref, strip_ref):
    members, variables = field_ref.shape[0], field_ref.shape[1]
    height, width = field_ref.shape[3], field_ref.shape[4]
    lane = lane_index((height, LANES))

    def edges(slot, v, rows):
        top_ref[slot, v, 0] = rows[:HALO]
        bottom_ref[slot, v, 0] = rows[height - HALO :]
        both = jnp.where(lane < HALO, rows[:, :LANES], rows[:, width - LANES :])
        return turn(both, HALO + 2 * HALO * v)

    for slot in range(members + 1):
        strip = jnp.zeros((height, LANES), jnp.float32)
        for v in range(variables):
            if slot < members:
                rows = field_ref[slot, v, 0] + kick_ref[slot, v, 0]
                start_ref[slot, v, 0] = rows
            else:
                rows = forcing_ref[v, 0]
            packed = edges(slot, v, rows)
            strip = jnp.where(lane >= 2 * HALO * v, packed, strip)
        strip_ref[slot, 0] = strip


def edges_of(field, kick, forcing):
    members, variables, levels, height, width = field.shape
    full = (members, variables, 1, height, width)
    slots = members + 1
    shape = jax.ShapeDtypeStruct
    return pl.pallas_call(
        edge_kernel,
        grid=(levels,),
        in_specs=[
            pl.BlockSpec(full, lambda k: (0, 0, k, 0, 0)),
            pl.BlockSpec(full, lambda k: (0, 0, k, 0, 0)),
            pl.BlockSpec((variables, 1, height, width), lambda k: (0, k, 0, 0)),
        ],
        out_specs=[
            pl.BlockSpec(full, lambda k: (0, 0, k, 0, 0)),
            pl.BlockSpec((slots, variables, 1, HALO, width), lambda k: (0, 0, k, 0, 0)),
            pl.BlockSpec((slots, variables, 1, HALO, width), lambda k: (0, 0, k, 0, 0)),
            pl.BlockSpec((slots, 1, height, LANES), lambda k: (0, k, 0, 0)),
        ],
        out_shape=[
            shape(field.shape, jnp.float32),
            shape((slots, variables, levels, HALO, width), jnp.float32),
            shape((slots, variables, levels, HALO, width), jnp.float32),
            shape((slots, levels, height, LANES), jnp.float32),
        ],
        compiler_params=pltpu.CompilerParams(vmem_limit_bytes=VMEM),
    )(field, kick, forcing)


def exchange(top, bottom, strip):
    lats, lons = lax.axis_size("lat"), lax.axis_size("lon")
    assert lons == 2
    south = [(i, i + 1) for i in range(lats - 1)]
    north = [(i + 1, i) for i in range(lats - 1)]

    def crossed(pairs):
        return [(a * lons + j, b * lons + 1 - j) for a, b in pairs for j in range(lons)]

    above = lax.ppermute(bottom, "lat", south)
    below = lax.ppermute(top, "lat", north)
    side = lax.ppermute(strip, "lon", [(0, 1), (1, 0)])
    side_above = lax.ppermute(strip[:, :, -HALO:], ("lat", "lon"), crossed(south))
    side_below = lax.ppermute(strip[:, :, :HALO], ("lat", "lon"), crossed(north))
    return above, below, side, side_above, side_below


def cut(rows, strip, v):
    width = rows.shape[1]
    count = -(-width // SPAN)
    lane = lane_index((rows.shape[0], LANES))
    source = [rows[:, LANES * t : LANES * (t + 1)] for t in range(width // LANES)]
    tiles = []
    for c in range(count):
        first = SPAN * c - HALO
        if c == 0:
            tile = jnp.where(lane < HALO, turn(strip, -2 * HALO * v), turn(source[0], HALO))
        else:
            t, offset = first // LANES, first % LANES
            if t + 1 < len(source):
                later = turn(source[t + 1], -offset)
            else:
                later = turn(strip, LANES - offset - 2 * HALO * v - HALO)
            tile = jnp.where(lane < LANES - offset, turn(source[t], -offset), later)
        tiles.append(tile)
    return tiles


def step_kernel(
    start_ref, above_ref, below_ref, side_ref, side_above_ref, side_below_ref,
    forcing_ref, f_above_ref, f_below_ref, f_side_ref, f_side_above_ref, f_side_below_ref,
    coupling_ref, place_ref, out_ref, cells, source, result,
):
    level = pl.program_id(0)
    variables, height, width = start_ref.shape[1], start_ref.shape[3], start_ref.shape[4]
    count = -(-width // SPAN)
    blocks = (height + 2 * HALO) // ROWS
    base = ROWS

    def lay(rows, strip, v, target, at, scale):
        for c, tile in enumerate(cut(rows, strip, v)):
            target[c, v, at : at + rows.shape[0]] = tile if scale is None else tile * scale

    for v in range(variables):
        lay(above_ref[0, v, 0], side_above_ref[0, 0], v, cells.at[0], base, None)
        lay(start_ref[0, v, 0], side_ref[0, 0], v, cells.at[0], base + HALO, None)
        lay(below_ref[0, v, 0], side_below_ref[0, 0], v, cells.at[0], base + HALO + height, None)

    @pl.when(pl.program_id(1) == 0)
    def _():
        for v in range(variables):
            lay(f_above_ref[0, v, 0], f_side_above_ref[0, 0], v, source, 0, 0.1)
            lay(forcing_ref[v, 0], f_side_ref[0, 0], v, source, HALO, 0.1)
            lay(f_below_ref[0, v, 0], f_side_below_ref[0, 0], v, source, HALO + height, 0.1)

    weight = [
        [
            0.25 * coupling_ref[level * variables * variables + v * variables + w]
            + (1.0 - 60.0 * K if v == w else 0.0)
            for w in range(variables)
        ]
        for v in range(variables)
    ]
    at_top = place_ref[0] == 0
    at_bottom = place_ref[0] == place_ref[1] - 1

    @pl.loop(0, count)
    def _(c):
        for step in range(STEPS):
            now, later = cells.at[step % 2, c], cells.at[(step + 1) % 2, c]
            last = step == STEPS - 1
            for r in range(1, blocks - 1) if last else range(blocks):
                at = base + ROWS * r
                centre = [now[v, at : at + ROWS] for v in range(variables)]
                ku, kv = K * centre[0], K * centre[1]
                eu, ev = 8.0 * ku, 8.0 * kv
                east, west, far_east, far_west = 16.0 * K - eu, 16.0 * K + eu, ku - K, -K - ku
                south, north, far_south, far_north = 16.0 * K - ev, 16.0 * K + ev, kv - K, -K - kv
                for v in range(variables):
                    q = centre[v]
                    total = source[c, v, ROWS * r : ROWS * (r + 1)]
                    for w in range(variables):
                        total += weight[v][w] * centre[w]
                    along = east * turn(q, -1) + west * turn(q, 1)
                    along += far_east * turn(q, -2) + far_west * turn(q, 2)
                    across = south * now[v, at + 1 : at + 1 + ROWS] + north * now[v, at - 1 : at - 1 + ROWS]
                    across += far_south * now[v, at + 2 : at + 2 + ROWS] + far_north * now[v, at - 2 : at - 2 + ROWS]
                    total += along + across
                    if last:
                        result[c, v, ROWS * (r - 1) : ROWS * r] = total
                    else:
                        if r == 0:
                            total = jnp.where(at_top, 0.0, total)
                        if r == blocks - 1:
                            total = jnp.where(at_bottom, 0.0, total)
                        later[v, at : at + ROWS] = total

    lane = lane_index((height, LANES))
    for v in range(variables):
        for t in range(width // LANES):
            c, offset = LANES * t // SPAN, LANES * t % SPAN
            left = turn(result[c, v], -(offset + HALO))
            if c + 1 < count:
                right = turn(result[c + 1, v], SPAN - offset - HALO)
                left = jnp.where(lane < SPAN - offset, left, right)
            out_ref[0, v, 0, :, LANES * t : LANES * (t + 1)] = left


def advance(start, halo, forcing, coupling):
    members, variables, levels, height, width = start.shape
    above, below, side, side_above, side_below = halo
    slots = above.shape[0]
    count = -(-width // SPAN)
    tall = height + 2 * HALO
    place = jnp.stack([lax.axis_index("lat"), jnp.int32(lax.axis_size("lat"))])

    def field(rows):
        return (
            pl.BlockSpec((1, variables, 1, rows, width), lambda k, m: (m, 0, k, 0, 0)),
            pl.BlockSpec((1, variables, 1, rows, width), lambda k, m: (slots - 1, 0, k, 0, 0)),
        )

    def strips(rows):
        return (
            pl.BlockSpec((1, 1, rows, LANES), lambda k, m: (m, k, 0, 0)),
            pl.BlockSpec((1, 1, rows, LANES), lambda k, m: (slots - 1, k, 0, 0)),
        )

    main, _ = field(height)
    edge, f_edge = field(HALO)
    flank, f_flank = strips(height)
    corner, f_corner = strips(HALO)
    scalars = pl.BlockSpec(memory_space=pltpu.SMEM)
    return pl.pallas_call(
        step_kernel,
        grid=(levels, members),
        in_specs=[
            main, edge, edge, flank, corner, corner,
            pl.BlockSpec((variables, 1, height, width), lambda k, m: (0, k, 0, 0)),
            f_edge, f_edge, f_flank, f_corner, f_corner,
            scalars, scalars,
        ],
        out_specs=main,
        out_shape=jax.ShapeDtypeStruct(start.shape, jnp.float32),
        scratch_shapes=[
            pltpu.VMEM((2, count, variables, tall + 2 * ROWS, LANES), jnp.float32),
            pltpu.VMEM((count, variables, tall, LANES), jnp.float32),
            pltpu.VMEM((count, variables, height, LANES), jnp.float32),
        ],
        compiler_params=pltpu.CompilerParams(vmem_limit_bytes=VMEM),
    )(
        start, above, below, side, side_above, side_below,
        forcing, above, below, side, side_above, side_below,
        coupling.reshape(-1), place,
    )


def shards(state, kick, forcing, coupling, clone_src):
    per_dev = state.shape[0]
    group = lax.axis_index("member")
    sources = lax.dynamic_slice_in_dim(clone_src, group * per_dev, per_dev)
    piece = lax.all_gather(state, "member", axis=0, tiled=True)
    field = jnp.take(piece, sources, axis=0, mode="clip")
    start, top, bottom, strip = edges_of(field, kick, forcing)
    halo = exchange(top, bottom, strip)
    return advance(start, halo, forcing, coupling)


def solution(mesh):
    in_specs = (
        P("member", None, None, "lat", "lon"),
        P("member", None, None, "lat", "lon"),
        P(None, None, "lat", "lon"),
        P(),
        P(),
    )
    out_specs = P("member", None, None, "lat", "lon")
    return jax.shard_map(shards, mesh=mesh, in_specs=in_specs, out_specs=out_specs, check_vma=False)
```

time: 212 us -> 154 us (0.73)
  matrix products: 24.9 us -> 0 us
  waiting for transfers between devices: 124 us -> 101 us
  Pallas kernels: 0 us -> 17.6 us
  other arithmetic: 16.9 us -> 0.08 us
  local copies, waits for them, and re-layouts: 16.4 us -> 5.67 us
    dot_general x4 -> x0, matrix products: 24.9 us -> none  [advance(): jnp.einsum('kvw,mwkij->mvkij', coupling, centre, precision=lax.Precision....]
    ppermute x16 -> x5, waiting for transfers between devices: 24.8 us -> 0.8 us  [the longest x1 0.76 us: exchange(): lax.ppermute(strip[:, :, -HALO:], ('lat', 'lon'), crossed(south))]
    pallas_call x0 -> x2, Pallas kernels: none -> 17.6 us  [the longest x1 16.1 us: advance(): pl.pallas_call(step_kernel, grid=(levels, members), in_specs=[main, edge,...]
    select_n x4 -> x0, other arithmetic: 5.13 us -> none  [zero_rows(): return jnp.where(keep[:, None], values, 0.0)]
    ppermute x8 -> x0, local copies, waits for them, and re-layouts: 4.95 us -> none  [the longest x4 3.54 us: with_halo(): lax.ppermute(lax.slice_in_dim(block, 0, width, axis=dim), axis, backward)]
    slice x12 -> x1, local copies, waits for them, and re-layouts: 4.91 us -> 0.01 us  [exchange(): strip[:, :, :HALO]]
    mul x5 -> x0, other arithmetic: 4.65 us -> none  [the longest x4 4.59 us: advance(): wind_u * along_x + wind_v * along_y]
    add x1 -> x0, other arithmetic: 3.87 us -> none  [shards(): field = field + kick]
  transfers between devices with their start and end apart: 17 -> 6, of which waited for: 16 -> 2; matrix products, arithmetic and copies ran while one was open for 2% -> 0% of each run, Pallas kernels for 0% -> 0%
where the time goes in v1:
time: 154 us; the launch traced here: 151 us
  waiting for transfers between devices  101 us (66%)
  Pallas kernels  17.6 us (11%)
  between operations  13.5 us (9%)
  starting transfers between devices  13.3 us (9%)
  local copies, waits for them, and re-layouts  5.67 us (4%)
    all_gather x1, waiting for transfers between devices, shards(): piece = lax.all_gather(state, 'member', axis=0, tiled=True)  99.1 us
    pallas_call x1, Pallas kernels, advance(): pl.pallas_call(step_kernel, grid=(levels, members), in_specs=[main, edge,...  16.1 us
    ppermute x1, starting transfers between devices, exchange(): lax.ppermute(strip[:, :, -HALO:], ('lat', 'lon'), crossed(south))  4.54 us
    ppermute x1, starting transfers between devices, exchange(): above = lax.ppermute(bottom, 'lat', south)  3.65 us
    gather x1, local copies, waits for them, and re-layouts, shards(): field = jnp.take(piece, sources, axis=0, mode='clip')  3.12 us
  transfers between devices with their start and end apart: 6, of which 2 were waited for; matrix products, arithmetic and copies ran while one was open for 0% of the time, Pallas kernels for 0%

profile of v1, /device:TPU:17, one launch (start us, length us, event | category | flops | bytes accessed | tf_op | source)
XLA Modules:
  0.0 150.8 jit_solution(2463839912730968461)
XLA Ops:
  6.5 0.0 copy-start.5
  6.5 0.0 all-gather.2.cloned.1.call-start
  6.5 0.7 all-gather.2.cloned.1.call-update
  7.3 0.0 copy-done.5
  7.3 0.1 dynamic_slice.3
  7.4 0.0 copy-start
  7.4 0.0 copy-start.1
  7.4 99.1 %all-gather.2.cloned.1.call-done = f32[8,5,2,32,512]{4,3,2,1,0:T(8,128)} async-done(((f32[2,5,2,32,512]{4,3,2,1,0:T(8,128)}), f32[8,5,2,32,512]{4,3,2,1,0:T(8,128)}) %all-gather.2.cloned.1.call-update) | async-done | bytes 5242896 | tf_op jit(solution)/shard_map/all_gather | solution.py:253
  106.5 3.1 %gather_fusion = f32[2,5,2,32,512]{4,3,2,1,0:T(8,128)S(1)} fusion(f32[8,5,2,32,512]{4,3,2,1,0:T(8,128)} %all-gather.2.cloned.1.call-done, s32[1024]{0:T(1024)S(1)} %pad_clamp_fusion), kind=kCustom, calls=%fused_computation | custom fusion | bytes 2621448 | tf_op jit(solution)/shard_map/jit(_take)/gather | solution.py:254
  109.6 0.0 copy-done
  109.6 0.0 copy-done.1
  109.6 0.0 copy-start.4
  109.6 1.5 %shard_map.55 = (f32[2,5,2,32,512]{4,3,2,1,0:T(8,128)S(1)}, f32[3,5,2,8,512]{4,3,2,1,0:T(8,128)}, f32[3,5,2,8,512]{4,3,2,1,0:T(8,128)}, f32[3,2,32,128]{3,2,1,0:T(8,128)S(1)}) custom-call(f32[2,5,2,32,512]{4,3,2,1,0:T(8,128)S(1)} %gather_fusion, f32[2,5,2,32,512]{4,3,2,1,0:T(8,128)S(1)} %copy-done.1, f32[5,2,32,512]{3,2,1,0:T(8,128)S(1)} %copy-done), custom_call_target="tpu_custom_call" | custom-call | tf_op jit(solution)/shard_map/pallas_call | solution.py:58
  111.1 0.0 copy-start.2
  111.1 1.1 copy-done.2
  112.2 3.6 %collective-permute-start = (f32[3,5,2,8,512]{4,3,2,1,0:T(8,128)}, f32[3,5,2,8,512]{4,3,2,1,0:T(8,128)S(1)}, u32[]{:S(2)}, u32[]{:S(2)}) collective-permute-start(f32[3,5,2,8,512]{4,3,2,1,0:T(8,128)} %get-tuple-element.10), channel_id=1, source_target_pairs={{0,2},{2,4},{4,6},{1,3},{3,5},{5,7},{8,10},{10,12},{12,14},{9,11},... | collective-permute-start | bytes 1474568 | tf_op jit(solution)/shard_map/ppermute | solution.py:91
  115.9 1.9 %collective-permute-start.1 = (f32[3,5,2,8,512]{4,3,2,1,0:T(8,128)}, f32[3,5,2,8,512]{4,3,2,1,0:T(8,128)S(1)}, u32[]{:S(2)}, u32[]{:S(2)}) collective-permute-start(f32[3,5,2,8,512]{4,3,2,1,0:T(8,128)} %get-tuple-element.11), channel_id=1, source_target_pairs={{2,0},{4,2},{6,4},{3,1},{5,3},{7,5},{10,8},{12,10},{14,12},{11,9},... | collective-permute-start | bytes 1474568 | tf_op jit(solution)/shard_map/ppermute | solution.py:92
  117.8 1.3 collective-permute-start.2
  119.1 1.9 %collective-permute-start.4 = (f32[3,2,8,128]{3,2,1,0:T(8,128)S(1)}, f32[3,2,8,128]{3,2,1,0:T(8,128)S(1)}, u32[]{:S(2)}, u32[]{:S(2)}) collective-permute-start(f32[3,2,8,128]{3,2,1,0:T(8,128)S(1)} %get-tuple-element.13), channel_id=1, source_target_pairs={{2,1},{3,0},{4,3},{5,2},{6,5},{7,4},{10,9},{11,8},{12,11},{13,10},... | collective-permute-start | bytes 73736 | tf_op jit(solution)/shard_map/ppermute | solution.py:95
  121.0 4.5 %collective-permute-start.3 = (f32[3,2,8,128]{3,2,1,0:T(8,128)S(1)}, f32[3,2,8,128]{3,2,1,0:T(8,128)S(1)}, u32[]{:S(2)}, u32[]{:S(2)}) collective-permute-start(f32[3,2,8,128]{3,2,1,0:T(8,128)S(1)} %get-tuple-element.14), channel_id=1, source_target_pairs={{0,3},{1,2},{2,5},{3,4},{4,7},{5,6},{8,11},{9,10},{10,13},{11,12},... | collective-permute-start | bytes 73736 | tf_op jit(solution)/shard_map/ppermute | solution.py:94
  125.5 0.1 pad_add_fusion.place_ref
  125.6 0.0 copy-done.4
  125.6 0.1 reshape.3.coupling_ref
  125.7 0.0 collective-permute-done.4.side_below_ref.f_side_below_ref
  125.7 0.8 collective-permute-done.3.side_above_ref.f_side_above_ref
  126.4 0.0 collective-permute-done.2.side_ref.f_side_ref
  126.4 0.0 collective-permute-done.above_ref.f_above_ref
  126.4 0.0 collective-permute-done.1.below_ref.f_below_ref
  126.5 0.0 copy-start.3
  126.5 1.3 copy-done.3
  127.8 16.1 %shard_map.56 = f32[2,5,2,32,512]{4,3,2,1,0:T(8,128)} custom-call(f32[2,5,2,32,512]{4,3,2,1,0:T(8,128)S(1)} %copy-done.3, f32[3,5,2,8,512]{4,3,2,1,0:T(8,128)S(1)} %collective-permute-done.above_ref.f_above_ref, f32[3,5,2,8,512]{4,3,2,1,0:T(8,128)S(1)} %collective-permute-done.1.below_ref.f_below_ref, ...), custom_call_target="tpu_custom_call" | custom-call | tf_op jit(solution)/shard_map/pallas_call | solution.py:225
  (3 shorter events, 0.0 us)
Async XLA Ops:
  6.5 0.7 copy-start.5
  6.5 99.9 %all-gather.2.cloned.1.call-start = ((), (), s32[]{:S(2)}) async-start(), calls=%async_computation | async-start | bytes 6553600 | tf_op jit(solution)/shard_map/all_gather | solution.py:253
  7.4 102.2 %copy-start = (f32[5,2,32,512]{3,2,1,0:T(8,128)S(1)}, f32[5,2,32,512]{3,2,1,0:T(8,128)}, u32[]{:S(2)}) copy-start(f32[5,2,32,512]{3,2,1,0:T(8,128)} %forcing_ref.3) | copy-start | bytes 1966084
  7.4 102.3 %copy-start.1 = (f32[2,5,2,32,512]{4,3,2,1,0:T(8,128)S(1)}, f32[2,5,2,32,512]{4,3,2,1,0:T(8,128)}, u32[]{:S(2)}) copy-start(f32[2,5,2,32,512]{4,3,2,1,0:T(8,128)} %kick_ref.1) | copy-start | bytes 3932164
  109.6 16.0 %copy-start.4 = (f32[2,5,5]{2,0,1:T(2,128)S(1)}, f32[2,5,5]{2,0,1:T(2,128)}, u32[]{:S(2)}) copy-start(f32[2,5,5]{2,0,1:T(2,128)} %param.8) | copy-start | bytes 604
  111.1 1.1 copy-start.2
  112.2 14.2 %collective-permute-start = (f32[3,5,2,8,512]{4,3,2,1,0:T(8,128)}, f32[3,5,2,8,512]{4,3,2,1,0:T(8,128)S(1)}, u32[]{:S(2)}, u32[]{:S(2)}) collective-permute-start(f32[3,5,2,8,512]{4,3,2,1,0:T(8,128)} %get-tuple-element.10), channel_id=1, source_target_pairs={{0,2},{2,4},{4,6},{1,3},{3,5},{5,7},{8,10},{10,12},{12,14},{9,11},... | collective-permute-start | bytes 1474568 | tf_op jit(solution)/shard_map/ppermute | solution.py:91
  115.9 10.6 %collective-permute-start.1 = (f32[3,5,2,8,512]{4,3,2,1,0:T(8,128)}, f32[3,5,2,8,512]{4,3,2,1,0:T(8,128)S(1)}, u32[]{:S(2)}, u32[]{:S(2)}) collective-permute-start(f32[3,5,2,8,512]{4,3,2,1,0:T(8,128)} %get-tuple-element.11), channel_id=1, source_target_pairs={{2,0},{4,2},{6,4},{3,1},{5,3},{7,5},{10,8},{12,10},{14,12},{11,9},... | collective-permute-start | bytes 1474568 | tf_op jit(solution)/shard_map/ppermute | solution.py:92
  117.8 8.7 %collective-permute-start.2 = (f32[3,2,32,128]{3,2,1,0:T(8,128)S(1)}, f32[3,2,32,128]{3,2,1,0:T(8,128)S(1)}, u32[]{:S(2)}, u32[]{:S(2)}) collective-permute-start(f32[3,2,32,128]{3,2,1,0:T(8,128)S(1)} %get-tuple-element.12), channel_id=1, source_target_pairs={{0,1},{1,0},{2,3},{3,2},{4,5},{5,4},{6,7},{7,6},{8,9},{9,8},{10,11... | collective-permute-start | bytes 294920 | tf_op jit(solution)/shard_map/ppermute | solution.py:93
  119.1 6.6 %collective-permute-start.4 = (f32[3,2,8,128]{3,2,1,0:T(8,128)S(1)}, f32[3,2,8,128]{3,2,1,0:T(8,128)S(1)}, u32[]{:S(2)}, u32[]{:S(2)}) collective-permute-start(f32[3,2,8,128]{3,2,1,0:T(8,128)S(1)} %get-tuple-element.13), channel_id=1, source_target_pairs={{2,1},{3,0},{4,3},{5,2},{6,5},{7,4},{10,9},{11,8},{12,11},{13,10},... | collective-permute-start | bytes 73736 | tf_op jit(solution)/shard_map/ppermute | solution.py:95
  121.0 5.5 %collective-permute-start.3 = (f32[3,2,8,128]{3,2,1,0:T(8,128)S(1)}, f32[3,2,8,128]{3,2,1,0:T(8,128)S(1)}, u32[]{:S(2)}, u32[]{:S(2)}) collective-permute-start(f32[3,2,8,128]{3,2,1,0:T(8,128)S(1)} %get-tuple-element.14), channel_id=1, source_target_pairs={{0,3},{1,2},{2,5},{3,4},{4,7},{5,6},{8,11},{9,10},{10,13},{11,12},... | collective-permute-start | bytes 73736 | tf_op jit(solution)/shard_map/ppermute | solution.py:94
  126.5 1.3 copy-start.3
Sparse Core Ops, SparseCore 0:
  8.9 97.5 all-gather.1
